TPU v7x, 32 devices: a whole 2x2x4 slice. The times are simulated.
32 devices in a mesh: parts: 2 (over y), row: 4 (over z), col: 4 (over x, core).
Axes of the slice: x: 2, y: 2, z: 4, core: 2. Of those that a mesh axis runs over, the one named last changes fastest.
Arguments:
- pair_acts: float32 [256, 128, 128], P(('parts', 'row'), 'col'), parts along dimension 0, may hold values from -6 to 6
- residue_mask: int32 [256], P('parts'), parts along dimension 0, may hold values 0 or 1
- norm_gain: float32 [128], replicated, may hold values from 0.1 to 1.9
- norm_bias: float32 [128], replicated, may hold values from -3 to 3
- w_left: bfloat16 [128, 256], replicated, may hold values from -0.5 to 0.5
- w_right: bfloat16 [128, 256], replicated, may hold values from -0.5 to 0.5
- w_gate: bfloat16 [128, 128], replicated, may hold values from -0.5 to 0.5
- out_gain: float32 [128], replicated, may hold values from 0.1 to 1.9
- out_bias: float32 [128], replicated, may hold values from -3 to 3
- w_out: bfloat16 [128, 128], replicated, may hold values from -0.5 to 0.5
Outputs:
- update: float32 [256, 128, 128], P(('parts', 'row'), 'col'), parts along dimension 0
There are 2 independent parts, one for each index of `parts`. A program takes and returns all parts, laid end to end along the dimension named above; an argument that names none is the same for every part. Nothing has to cross between parts.
All inputs are finite; a program needn't handle non-finite values.
Results may differ from a plain program's by a relative error of at most 0.0042.
Values may be sent and summed in bfloat16 or wider, within the bound.
A program may use at most 128 MiB of HBM per device.

v0:
```python
import jax
import jax.numpy as jnp
from jax import lax
from jax.sharding import PartitionSpec as P


def from_root(block, axis, holder):
    block = jnp.where(lax.axis_index(axis) == holder, block, jnp.zeros_like(block))
    return lax.psum(block, axis)


def layer_norm(values, gain, bias):
    mean = jnp.mean(values, axis=-1, keepdims=True)
    centred = values - mean
    var = jnp.mean(centred * centred, axis=-1, keepdims=True)
    return centred * lax.rsqrt(var + 1e-05) * gain + bias


def gated_side(flat_normed, weight, flat_mask, shape):
    both = jnp.dot(flat_normed, weight, preferred_element_type=jnp.float32)
    hidden = weight.shape[1] // 2
    act = jax.nn.sigmoid(both[:, hidden:]) * both[:, :hidden] * flat_mask
    return act.astype(jnp.bfloat16).reshape(shape)


def body(
    pair_acts,
    residue_mask,
    norm_gain,
    norm_bias,
    w_left,
    w_right,
    w_gate,
    out_gain,
    out_bias,
    w_out,
):
    row_count, col_count, channels = pair_acts.shape
    hidden = w_out.shape[0]
    normed = layer_norm(pair_acts, norm_gain, norm_bias).astype(jnp.bfloat16)
    flat_normed = normed.reshape(row_count * col_count, channels)
    valid = residue_mask.astype(jnp.float32)
    row_valid = lax.dynamic_slice_in_dim(valid, lax.axis_index("row") * row_count, row_count, 0)
    col_valid = lax.dynamic_slice_in_dim(valid, lax.axis_index("col") * col_count, col_count, 0)
    flat_mask = (row_valid[:, None] * col_valid[None, :]).reshape(row_count * col_count, 1)
    block_shape = (row_count, col_count, hidden)
    left_act = gated_side(flat_normed, w_left, flat_mask, block_shape)
    right_act = gated_side(flat_normed, w_right, flat_mask, block_shape)
    left_all, right_all = (
        lax.all_gather(left_act, "col", axis=1, tiled=True),
        lax.all_gather(right_act, "col", axis=1, tiled=True),
    )
    ratio = lax.axis_size("row") // lax.axis_size("col")
    owned = []
    for offset in range(ratio):
        owner = ratio * lax.axis_index("col") + offset
        owned.append(from_root(right_all, "row", owner))
    right_cols = jnp.concatenate(owned, axis=0)
    triangle = jnp.einsum("ikh,jkh->ijh", left_all, right_cols, preferred_element_type=jnp.float32)
    tri_norm = layer_norm(triangle, out_gain, out_bias).astype(jnp.bfloat16)
    gate = jax.nn.sigmoid(jnp.dot(flat_normed, w_gate, preferred_element_type=jnp.float32))
    projected = jnp.dot(
        tri_norm.reshape(row_count * col_count, hidden), w_out, preferred_element_type=jnp.float32
    )
    return (gate * projected).reshape(row_count, col_count, channels)


def solution(mesh):
    placed = (P(("parts", "row"), "col", None), P("parts"), P(), P(), P(), P(), P(), P(), P(), P())
    return jax.shard_map(
        body,
        mesh=mesh,
        in_specs=placed,
        out_specs=P(("parts", "row"), "col", None),
        check_vma=False,
    )
```

profile of v0, /device:TPU:3, one launch (start us, length us, event | category | flops | bytes accessed | tf_op | source)
XLA Modules:
  0.0 115.9 jit_solution(7654674778841579241)
XLA Ops:
  6.5 0.7 convert_element_type.16
  7.2 0.1 fusion.13
  7.3 0.1 broadcast_multiply_fusion
  7.4 0.1 mul.98
  7.5 1.2 %reduce_sum.36 = f32[32,32]{1,0:T(8,128)S(1)} reduce(f32[32,32,128]{2,1,0:T(8,128)} %param.10, f32[]{:T(128)} %constant.8.clone.1), dimensions={2}, to_apply=%region_0.0 | reduce | flops 130048 | bytes 528388 | tf_op jit(solution)/shard_map/reduce_sum | solution.py:13
  8.7 1.4 %multiply_reduce_fusion.1 = f32[32,32]{1,0:T(8,128)S(1)} fusion(f32[32,32,128]{2,1,0:T(8,128)} %param.10, f32[32,32]{1,0:T(8,128)S(1)} %broadcast_multiply_fusion.2), kind=kLoop, calls=%fused_computation.25 | loop fusion | flops 392192 | bytes 532480 | tf_op jit(solution)/shard_map/reduce_sum | solution.py:15
  10.2 1.4 %add_convert_fusion.1 = bf16[32,32,128]{2,1,0:T(8,128)(2,1)S(1)} fusion(f32[32,32,128]{2,1,0:T(8,128)} %param.10, f32[128]{0:T(128)} %param.13, f32[128]{0:T(128)} %param.12, f32[32,32]{1,0:T(8,128)S(1)} %add_rsqrt_fusion.1, f32[32,32]{1,0:T(8,128)S(1)} %broadcast_multiply_fusion.2), kind=kLoop, calls=%fused_computation.24 | loop fusion | flops 655360 | bytes 795648 | tf_op jit(solution)/shard_map/convert_element_type | solution.py:40
  11.6 0.3 fusion.14
  11.9 0.3 fusion.15
  12.1 0.3 fusion.4
  12.5 0.8 copy.36
  13.3 0.8 copy.38
  14.2 16.4 %all-gather.3.cloned.1.call-done = bf16[32,128,128]{2,0,1:T(8,128)(2,1)} async-done(((bf16[32,32,128]{2,0,1:T(8,128)(2,1)}), bf16[32,128,128]{2,0,1:T(8,128)(2,1)}) %all-gather.3.cloned.1.call-update) | async-done | bytes 1048592 | tf_op jit(solution)/shard_map/all_gather | solution.py:51
  30.7 2.5 %copy.37 = bf16[32,128,128]{1,0,2:T(8,128)(2,1)S(1)} copy(bf16[32,128,128]{2,0,1:T(8,128)(2,1)} %all-gather.3.cloned.1.call-done) | data formatting | bytes 2097152 | tf_op jit(solution)/shard_map/all_gather | solution.py:51
  33.1 1.1 broadcast_select_fusion
  34.2 1.1 fusion.2
  35.3 13.6 %all-gather.5.cloned.1.call-done = bf16[32,128,128]{2,0,1:T(8,128)(2,1)} async-done(((bf16[32,32,128]{2,0,1:T(8,128)(2,1)}), bf16[32,128,128]{2,0,1:T(8,128)(2,1)}) %all-gather.5.cloned.1.call-update) | async-done | bytes 1048592 | tf_op jit(solution)/shard_map/all_gather | solution.py:50
  49.0 2.5 %copy.39 = bf16[32,128,128]{1,0,2:T(8,128)(2,1)S(1)} copy(bf16[32,128,128]{2,0,1:T(8,128)(2,1)} %all-gather.5.cloned.1.call-done) | data formatting | bytes 2097152 | tf_op jit(solution)/shard_map/all_gather | solution.py:50
  51.4 52.7 %all-reduce.2.cloned.1.call-done = bf16[32,128,128]{1,0,2:T(8,128)(2,1)} async-done(((bf16[32,128,128]{1,0,2:T(8,128)(2,1)}), bf16[32,128,128]{1,0,2:T(8,128)(2,1)}) %all-reduce.2.cloned.1.call-update) | async-done | bytes 1048592 | tf_op jit(solution)/shard_map/psum | solution.py:9
  104.2 1.9 %bitcast_reduce_fusion = (f32[32,32]{0,1:T(8,128)S(1)}, f32[128,32,32]{2,1,0:T(8,128)S(1)}) fusion(bf16[32,128,128]{1,0,2:T(8,128)(2,1)} %all-reduce.2.cloned.1.call-done, bf16[32,128,128]{1,0,2:T(8,128)(2,1)S(1)} %copy.39), kind=kOutput, calls=%fused_computation | convolution fusion | flops 33684480 | bytes 2625536 | tf_op jit(solution)/shard_map/ikh,jkh->ijh/dot_general | solution.py:59
  106.1 1.4 %copy.40 = f32[128,32,32]{0,1,2:T(8,128)S(1)} copy(f32[128,32,32]{2,1,0:T(8,128)S(1)} %get-tuple-element.10) | data formatting | bytes 1048576 | tf_op jit(solution)/shard_map/ikh,jkh->ijh/dot_general | solution.py:59
  107.6 0.4 multiply_reduce_fusion
  108.1 0.3 add_convert_fusion
  108.4 1.0 convolution_multiply_fusion
  (25 shorter events, 0.3 us)
Async XLA Ops:
  6.5 5.0 %copy-start = (bf16[128,256]{1,0:T(8,128)(2,1)S(1)}, bf16[128,256]{1,0:T(8,128)(2,1)}, u32[]{:S(2)}) copy-start(bf16[128,256]{1,0:T(8,128)(2,1)} %param.15) | copy-start | bytes 196612
  6.5 5.3 %copy-start.2 = (bf16[128,256]{1,0:T(8,128)(2,1)S(1)}, bf16[128,256]{1,0:T(8,128)(2,1)}, u32[]{:S(2)}) copy-start(bf16[128,256]{1,0:T(8,128)(2,1)} %param.14) | copy-start | bytes 196612
  6.5 24.1 %all-gather.3.cloned.1.call-start = ((), (), s32[]{:S(2)}) async-start(), calls=%async_computation | async-start | bytes 1310720 | tf_op jit(solution)/shard_map/all_gather | solution.py:51
  13.3 35.7 %all-gather.5.cloned.1.call-start = ((), (), s32[]{:S(2)}) async-start(), calls=%async_computation.2 | async-start | bytes 1310720 | tf_op jit(solution)/shard_map/all_gather | solution.py:50
  14.2 90.0 %all-reduce.2.cloned.1.call-start = ((), (), s32[]{:S(2)}) async-start(), calls=%async_computation.1 | async-start | bytes 2097152 | tf_op jit(solution)/shard_map/psum | solution.py:9
  33.1 1.1 copy-start.6
  106.1 2.0 %copy-start.4 = (f32[128]{0:T(128)S(1)}, f32[128]{0:T(128)}, u32[]{:S(2)}) copy-start(f32[128]{0:T(128)} %param.18) | copy-start | bytes 1540
  106.1 2.0 %copy-start.5 = (f32[128]{0:T(128)S(1)}, f32[128]{0:T(128)}, u32[]{:S(2)}) copy-start(f32[128]{0:T(128)} %param.17) | copy-start | bytes 1540
  106.1 2.3 %copy-start.1 = (f32[1024,128]{1,0:T(8,128)S(1)}, f32[1024,128]{1,0:T(8,128)}, u32[]{:S(2)}) copy-start(f32[1024,128]{1,0:T(8,128)} %fusion.2) | copy-start | bytes 1572868
  106.1 2.3 %copy-start.3 = (bf16[128,128]{1,0:T(8,128)(2,1)S(1)}, bf16[128,128]{1,0:T(8,128)(2,1)}, u32[]{:S(2)}) copy-start(bf16[128,128]{1,0:T(8,128)(2,1)} %param.19) | copy-start | bytes 98308
Sparse Core Ops, SparseCore 0:
  13.4 17.1 all-gather.2
  32.2 16.7 all-gather.4
  51.3 52.7 all-reduce.1
where the time goes:
time: 118 us; the launch traced here: 116 us
  waiting for transfers between devices  82.8 us (70%)
  between operations  13.3 us (11%)
  local copies, waits for them, and re-layouts  8.23 us (7%)
  other arithmetic  6.97 us (6%)
  matrix products  4.52 us (4%)
    psum x1, waiting for transfers between devices, from_root(): return lax.psum(block, axis)  52.7 us
    all_gather x1, waiting for transfers between devices, body(): lax.all_gather(right_act, 'col', axis=1, tiled=True)  16.4 us
    all_gather x1, waiting for transfers between devices, body(): lax.all_gather(left_act, 'col', axis=1, tiled=True)  13.6 us
    all_gather x1, local copies, waits for them, and re-layouts, body(): lax.all_gather(right_act, 'col', axis=1, tiled=True)  2.47 us
    all_gather x1, local copies, waits for them, and re-layouts, body(): lax.all_gather(left_act, 'col', axis=1, tiled=True)  2.47 us
  transfers between devices with their start and end apart: 3, of which 3 were waited for; matrix products, arithmetic and copies ran while one was open for 7% of the time, Pallas kernels for 0%

commit v1 on v0

v1 whole, which is shorter than its diff:
```python
import functools

import jax
import jax.numpy as jnp
from jax import lax
from jax.experimental import pallas as pl
from jax.experimental.pallas import tpu as pltpu
from jax.sharding import PartitionSpec as P

F32 = jnp.float32
BF16 = jnp.bfloat16
PIECES = 4
GROUP = 8


def layer_norm(values, gain, bias):
    mean = jnp.mean(values, axis=-1, keepdims=True)
    centred = values - mean
    var = jnp.mean(centred * centred, axis=-1, keepdims=True)
    return centred * lax.rsqrt(var + 1e-05) * gain + bias


def sigmoid(values):
    return 0.5 * jnp.tanh(0.5 * values) + 0.5


def kernel(
    rows,
    cols,
    mask_ref,
    x_ref,
    gain_ref,
    bias_ref,
    w_left_ref,
    w_right_ref,
    w_gate_ref,
    out_gain_ref,
    out_bias_ref,
    w_out_ref,
    out_ref,
    chain,
    right,
    left,
    left32,
    tri,
    gate,
    row_valid,
    up_send,
    up_recv,
    down_send,
    down_recv,
    swap_send,
    swap_recv,
    far_send,
    pair_send,
    left_recv,
):
    z = lax.axis_index("row")
    c = lax.axis_index("col")
    x, core = c // 2, c % 2
    twin = 2 * x + 1 - core
    chips = cols // 2
    ratio = rows // cols
    k_count, i_count, hidden = chain.shape[1:]
    piece = k_count // PIECES
    j_count = ratio * i_count

    barrier = pltpu.get_barrier_semaphore()

    @pl.when(z > 0)
    def _():
        pl.semaphore_signal(barrier, inc=1, device_id={"row": z - 1}, device_id_type=pl.DeviceIdType.MESH)

    @pl.when(z < rows - 1)
    def _():
        pl.semaphore_signal(barrier, inc=1, device_id={"row": z + 1}, device_id_type=pl.DeviceIdType.MESH)

    for step in range(1, cols):
        pl.semaphore_signal(
            barrier, inc=1, device_id={"col": lax.rem(c + step, cols)}, device_id_type=pl.DeviceIdType.MESH
        )

    def part(p):
        return pl.ds(p * piece, piece)

    def up(step, p, block):
        ref = chain.at[block, part(p)]
        return pltpu.make_async_remote_copy(
            ref, ref, up_send.at[step, p], up_recv.at[step, p], {"row": z + 1}, pl.DeviceIdType.MESH
        )

    def down(step, p, block):
        ref = chain.at[block, part(p)]
        return pltpu.make_async_remote_copy(
            ref, ref, down_send.at[step, p], down_recv.at[step, p], {"row": z - 1}, pl.DeviceIdType.MESH
        )

    def swap(p, block):
        return pltpu.make_async_remote_copy(
            chain.at[block, part(p)],
            right.at[c, block % ratio, part(p)],
            swap_send.at[block, p],
            swap_recv.at[c, block % ratio, p],
            {"col": block // ratio},
            pl.DeviceIdType.MESH,
        )

    def keep(p, block):
        return pltpu.make_async_copy(
            chain.at[block, part(p)], right.at[c, block % ratio, part(p)], swap_recv.at[c, block % ratio, p]
        )

    def deliver(p, block):
        @pl.when(block // ratio != c)
        def _():
            swap(p, block).start()

        @pl.when(block // ratio == c)
        def _():
            keep(p, block).start()

    def left_copy(p, owner, target, send):
        ref = left.at[owner, part(p)]
        return pltpu.make_async_remote_copy(
            ref, ref, send, left_recv.at[owner, p], {"col": target}, pl.DeviceIdType.MESH
        )

    def far(p, step):
        return left_copy(p, c, 2 * lax.rem(x + step, chips) + core, far_send.at[step - 1, p])

    def pair(p, step):
        return left_copy(p, 2 * lax.rem(x + step, chips) + core, twin, pair_send.at[step, p])

    for i in range(i_count):
        row_valid[pl.ds(i, 1), :] = jnp.full((1, hidden), mask_ref[z * i_count + i].astype(F32))

    def side(normed, weight, mask):
        both = jnp.dot(normed, weight, preferred_element_type=F32)
        act = sigmoid(both[:, hidden:]) * both[:, :hidden] * mask
        return act.astype(BF16).reshape(piece, i_count, hidden)

    gain, bias = gain_ref[...], bias_ref[...]
    for p in range(PIECES):
        values = jnp.concatenate(
            [x_ref[pl.ds(p * piece + k, i_count, stride=k_count), :] for k in range(piece)], axis=0
        )
        mask = jnp.concatenate(
            [row_valid[...] * mask_ref[c * k_count + p * piece + k].astype(F32) for k in range(piece)], axis=0
        )
        normed = layer_norm(values, gain, bias).astype(BF16)
        chain[z, part(p)] = side(normed, w_right_ref[...], mask)
        if p == 0:
            neighbours = cols - 1 + (z > 0).astype(jnp.int32) + (z < rows - 1).astype(jnp.int32)
            pl.semaphore_wait(barrier, neighbours)

        @pl.when(z < rows - 1)
        def _():
            up(0, p, z).start()

        @pl.when(z > 0)
        def _():
            down(0, p, z).start()

        left[c, part(p)] = side(normed, w_left_ref[...], mask)
        for step in range(1, chips):
            far(p, step).start()
        pair(p, 0).start()
        deliver(p, z)

    tri[...] = jnp.zeros_like(tri)
    flat = GROUP * k_count

    def make_gate(g, carry):
        span = pl.ds(pl.multiple_of(g * flat, flat), flat)
        normed = layer_norm(x_ref[span, :], gain, bias).astype(BF16)
        gate[span, :] = sigmoid(jnp.dot(normed, w_gate_ref[...], preferred_element_type=F32))
        return carry

    lax.fori_loop(0, i_count // GROUP, make_gate, 0)

    def relay(step, p):
        @pl.when(z - 1 - step >= 0)
        def _():
            up(step, p, z - 1 - step).wait_recv()
            if step < rows - 2:

                @pl.when(z < rows - 1)
                def _():
                    up(step + 1, p, z - 1 - step).start()

            deliver(p, z - 1 - step)

        @pl.when(z + 1 + step < rows)
        def _():
            down(step, p, z + 1 + step).wait_recv()
            if step < rows - 2:

                @pl.when(z > 0)
                def _():
                    down(step + 1, p, z + 1 + step).start()

            deliver(p, z + 1 + step)

        if step == 0:
            for other in range(1, chips):
                pair(p, other).wait_recv()
                pair(p, other).start()

    def multiply(p):
        for owner in range(cols):
            for offset in range(ratio):
                ref = right.at[owner, offset, part(p)]
                pltpu.make_async_copy(ref, ref, swap_recv.at[owner, offset, p]).wait()
        for other in range(chips):
            owner = 2 * lax.rem(x + other, chips) + 1 - core
            left_copy(p, owner, twin, pair_send.at[other, p]).wait_recv()

        def widen(owner, carry):
            left32[pl.ds(owner * piece, piece)] = left[owner, part(p)].astype(F32)
            return carry

        lax.fori_loop(0, cols, widen, 0)
        groups = i_count // GROUP

        def block(at, carry):
            offset, first = at // groups, pl.multiple_of((at % groups) * GROUP, GROUP)
            js = pl.ds(pl.multiple_of(offset * i_count, i_count), i_count)

            def add(owner, sums):
                for k in range(piece):
                    other = right[owner, offset, p * piece + k].astype(F32)
                    sums = tuple(
                        total + left32[owner * piece + k, pl.ds(first + g, 1), :] * other
                        for g, total in enumerate(sums)
                    )
                return sums

            sums = tuple(tri[first + g, js, :] for g in range(GROUP))
            sums = lax.fori_loop(0, cols, add, sums)
            for g in range(GROUP):
                tri[first + g, js, :] = sums[g]
            return carry

        lax.fori_loop(0, groups * ratio, block, 0)

    for step in range(rows - 2):
        for p in range(PIECES):
            relay(step, p)
    for p in range(PIECES):
        relay(rows - 2, p)
        if p > 0:
            multiply(p - 1)
    multiply(PIECES - 1)

    def finish(g, carry):
        span = pl.ds(pl.multiple_of(g * flat, flat), flat)
        values = tri[pl.ds(g * GROUP, GROUP)].reshape(flat, hidden)
        normed = layer_norm(values, out_gain_ref[...], out_bias_ref[...]).astype(BF16)
        out_ref[span, :] = gate[span, :] * jnp.dot(normed, w_out_ref[...], preferred_element_type=F32)
        return carry

    lax.fori_loop(0, i_count // GROUP, finish, 0)

    for p in range(PIECES):
        for step in range(rows - 1):

            @pl.when((z < rows - 1) & (z - step >= 0))
            def _():
                up(step, p, z - step).wait_send()

            @pl.when((z > 0) & (z + step < rows))
            def _():
                down(step, p, z + step).wait_send()

        for step in range(1, chips):
            far(p, step).wait_send()
        for step in range(chips):
            pair(p, step).wait_send()
        for block in range(rows):

            @pl.when(block // ratio != c)
            def _():
                swap(p, block).wait_send()


def solution(mesh):
    rows, cols = mesh.shape["row"], mesh.shape["col"]

    def body(pair_acts, residue_mask, norm_gain, norm_bias, w_left, w_right, w_gate, out_gain, out_bias, w_out):
        i_count, k_count, channels = pair_acts.shape
        hidden = w_out.shape[0]
        ratio = rows // cols
        piece = k_count // PIECES
        dma = pltpu.SemaphoreType.DMA
        vmem = pl.BlockSpec(memory_space=pltpu.VMEM)
        flat = pl.pallas_call(
            functools.partial(kernel, rows, cols),
            out_shape=jax.ShapeDtypeStruct((i_count * k_count, channels), F32),
            in_specs=[pl.BlockSpec(memory_space=pltpu.SMEM)] + [vmem] * 9,
            out_specs=vmem,
            scratch_shapes=[
                pltpu.VMEM((rows, k_count, i_count, hidden), BF16),
                pltpu.VMEM((cols, ratio, k_count, i_count, hidden), BF16),
                pltpu.VMEM((cols, k_count, i_count, hidden), BF16),
                pltpu.VMEM((cols * piece, i_count, hidden), F32),
                pltpu.VMEM((i_count, k_count, hidden), F32),
                pltpu.VMEM((i_count * k_count, channels), F32),
                pltpu.VMEM((i_count, hidden), F32),
                dma((rows - 1, PIECES)),
                dma((rows - 1, PIECES)),
                dma((rows - 1, PIECES)),
                dma((rows - 1, PIECES)),
                dma((rows, PIECES)),
                dma((cols, ratio, PIECES)),
                dma((cols // 2 - 1, PIECES)),
                dma((cols // 2, PIECES)),
                dma((cols, PIECES)),
            ],
            compiler_params=pltpu.CompilerParams(
                collective_id=0, has_side_effects=True, vmem_limit_bytes=48 * 1024 * 1024
            ),
        )(
            residue_mask,
            pair_acts.reshape(i_count * k_count, channels),
            norm_gain.reshape(1, channels),
            norm_bias.reshape(1, channels),
            w_left,
            w_right,
            w_gate,
            out_gain.reshape(1, hidden),
            out_bias.reshape(1, hidden),
            w_out,
        )
        return flat.reshape(i_count, k_count, channels)

    placed = (P(("parts", "row"), "col", None), P("parts"), P(), P(), P(), P(), P(), P(), P(), P())
    return jax.shard_map(
        body,
        mesh=mesh,
        in_specs=placed,
        out_specs=P(("parts", "row"), "col", None),
        check_vma=False,
    )
```

time: 118 us -> 38.6 us (0.33)
  the two profiles are of different devices: /device:TPU:3 before, /device:TPU:24 now
where the time goes in v1:
time: 38.6 us; the launch traced here: 38.2 us
  Pallas kernels  32.5 us (84%)
  local copies, waits for them, and re-layouts  5.73 us (15%)
    pallas_call x1, Pallas kernels, body(): pl.pallas_call(functools.partial(kernel, rows, cols), out_shape=jax.Shape...  32.5 us
    unnamed x21, local copies, waits for them, and re-layouts  5.73 us

profile of v1, /device:TPU:24, one launch (start us, length us, event | category | flops | bytes accessed | tf_op | source)
XLA Modules:
  0.0 38.2 jit_solution(8476859929170367620)
XLA Ops:
  0.0 0.0 copy-start.8
  0.0 0.0 copy-start.9
  0.0 0.0 copy-start.5
  0.0 0.0 copy-start.6
  0.0 0.0 copy-start.7
  0.0 0.6 %copy-done.8 = f32[128]{0:T(128)S(1)} copy-done((f32[128]{0:T(128)S(1)}, f32[128]{0:T(128)}, u32[]{:S(2)}) %copy-start.8) | copy-done | bytes 536
  0.7 0.0 copy-done.9
  0.7 0.0 copy-done.5
  0.7 0.0 copy-done.6
  0.7 0.0 copy-done.7
  0.7 0.0 copy-start
  0.7 1.0 %copy-done = f32[32,32,128]{2,1,0:T(8,128)S(1)} copy-done((f32[32,32,128]{2,1,0:T(8,128)S(1)}, f32[32,32,128]{2,1,0:T(8,128)}, u32[]{:S(2)}) %copy-start) | copy-done | bytes 524312
  1.8 0.0 copy-start.1
  1.8 0.8 %copy-done.1 = bf16[128,256]{1,0:T(8,128)(2,1)S(1)} copy-done((bf16[128,256]{1,0:T(8,128)(2,1)S(1)}, bf16[128,256]{1,0:T(8,128)(2,1)}, u32[]{:S(2)}) %copy-start.1) | copy-done | bytes 65560
  2.6 0.0 copy-start.2
  2.6 0.8 %copy-done.2 = bf16[128,256]{1,0:T(8,128)(2,1)S(1)} copy-done((bf16[128,256]{1,0:T(8,128)(2,1)S(1)}, bf16[128,256]{1,0:T(8,128)(2,1)}, u32[]{:S(2)}) %copy-start.2) | copy-done | bytes 65560
  3.4 0.0 copy-start.3
  3.4 0.8 %copy-done.3 = bf16[128,128]{1,0:T(8,128)(2,1)S(1)} copy-done((bf16[128,128]{1,0:T(8,128)(2,1)S(1)}, bf16[128,128]{1,0:T(8,128)(2,1)}, u32[]{:S(2)}) %copy-start.3) | copy-done | bytes 32792
  4.2 0.0 copy-start.4
  4.2 0.8 %copy-done.4 = bf16[128,128]{1,0:T(8,128)(2,1)S(1)} copy-done((bf16[128,128]{1,0:T(8,128)(2,1)S(1)}, bf16[128,128]{1,0:T(8,128)(2,1)}, u32[]{:S(2)}) %copy-start.4) | copy-done | bytes 32792
  5.0 32.5 %shard_map.100 = f32[1024,128]{1,0:T(8,128)S(1)} custom-call(s32[128]{0:T(128)S(1)} %copy-done.5, f32[1024,128]{1,0:T(8,128)S(1)} %bitcast.7, f32[1,128]{1,0:T(1,128)S(1)} %bitcast.8, f32[1,128]{1,0:T(1,128)S(1)} %bitcast.9, bf16[128,256]{1,0:T(8,128)(2,1)S(1)} %copy-done.1, bf16[128,256]{1,0:T(8,128)(2,1)S(1)} %copy-done.2, bf16[128,128]{1,0:T(8,128)(2,1)S(1)} %copy-done.3, ...), custom_call_target="tpu_custom_call" | custom-call | tf_op jit(solution)/shard_map/pallas_call | solution.py:296
  37.4 0.8 %copy.12 = f32[32,32,128]{2,1,0:T(8,128)} copy(f32[32,32,128]{2,1,0:T(8,128)S(1)} %bitcast.6) | data formatting | bytes 1048576
Async XLA Ops:
  0.0 0.7 %copy-start.8 = (f32[128]{0:T(128)S(1)}, f32[128]{0:T(128)}, u32[]{:S(2)}) copy-start(f32[128]{0:T(128)} %param.17) | copy-start | bytes 1540
  0.0 0.7 %copy-start.9 = (f32[128]{0:T(128)S(1)}, f32[128]{0:T(128)}, u32[]{:S(2)}) copy-start(f32[128]{0:T(128)} %param.18) | copy-start | bytes 1540
  0.0 0.7 %copy-start.5 = (s32[128]{0:T(128)S(1)}, s32[128]{0:T(128)}, u32[]{:S(2)}) copy-start(s32[128]{0:T(128)} %mask_ref.1) | copy-start | bytes 1540
  0.0 0.7 %copy-start.6 = (f32[128]{0:T(128)S(1)}, f32[128]{0:T(128)}, u32[]{:S(2)}) copy-start(f32[128]{0:T(128)} %param.12) | copy-start | bytes 1540
  0.0 0.7 %copy-start.7 = (f32[128]{0:T(128)S(1)}, f32[128]{0:T(128)}, u32[]{:S(2)}) copy-start(f32[128]{0:T(128)} %param.13) | copy-start | bytes 1540
  0.7 1.0 %copy-start = (f32[32,32,128]{2,1,0:T(8,128)S(1)}, f32[32,32,128]{2,1,0:T(8,128)}, u32[]{:S(2)}) copy-start(f32[32,32,128]{2,1,0:T(8,128)} %param.10) | copy-start | bytes 1572868
  1.8 0.8 %copy-start.1 = (bf16[128,256]{1,0:T(8,128)(2,1)S(1)}, bf16[128,256]{1,0:T(8,128)(2,1)}, u32[]{:S(2)}) copy-start(bf16[128,256]{1,0:T(8,128)(2,1)} %w_left_ref.1) | copy-start | bytes 196612
  2.6 0.8 %copy-start.2 = (bf16[128,256]{1,0:T(8,128)(2,1)S(1)}, bf16[128,256]{1,0:T(8,128)(2,1)}, u32[]{:S(2)}) copy-start(bf16[128,256]{1,0:T(8,128)(2,1)} %w_right_ref.1) | copy-start | bytes 196612
  3.4 0.8 %copy-start.3 = (bf16[128,128]{1,0:T(8,128)(2,1)S(1)}, bf16[128,128]{1,0:T(8,128)(2,1)}, u32[]{:S(2)}) copy-start(bf16[128,128]{1,0:T(8,128)(2,1)} %w_gate_ref.1) | copy-start | bytes 98308
  4.2 0.8 %copy-start.4 = (bf16[128,128]{1,0:T(8,128)(2,1)S(1)}, bf16[128,128]{1,0:T(8,128)(2,1)}, u32[]{:S(2)}) copy-start(bf16[128,128]{1,0:T(8,128)(2,1)} %w_out_ref.1) | copy-start | bytes 98308

commit v2 on v1

--- a/solution.py
+++ b/solution.py
@@ -27,34 +27,46 @@
 def kernel(
     rows,
     cols,
-    mask_ref,
-    x_ref,
-    gain_ref,
-    bias_ref,
-    w_left_ref,
-    w_right_ref,
-    w_gate_ref,
-    out_gain_ref,
-    out_bias_ref,
-    w_out_ref,
-    out_ref,
-    chain,
-    right,
-    left,
-    left32,
-    tri,
-    gate,
-    row_valid,
-    up_send,
-    up_recv,
-    down_send,
-    down_recv,
-    swap_send,
-    swap_recv,
-    far_send,
-    pair_send,
-    left_recv,
+    *refs,
 ):
+    sources, out_ref, held = refs[:10], refs[10], refs[11:21]
+    (
+        mask_ref,
+        x_ref,
+        gain_ref,
+        bias_ref,
+        w_left_ref,
+        w_right_ref,
+        w_gate_ref,
+        out_gain_ref,
+        out_bias_ref,
+        w_out_ref,
+    ) = held
+    (
+        chain,
+        right,
+        left,
+        left32,
+        tri,
+        gate,
+        row_valid,
+        up_send,
+        up_recv,
+        down_send,
+        down_recv,
+        swap_send,
+        swap_recv,
+        far_send,
+        pair_send,
+        left_recv,
+        load_sem,
+    ) = refs[21:]
+    loads = [
+        pltpu.make_async_copy(source, target, load_sem.at[at])
+        for at, (source, target) in enumerate(zip(sources, held))
+    ]
+    for at in (1, 0, 5, 2, 3, 4, 6, 7, 8, 9):
+        loads[at].start()
     z = lax.axis_index("row")
     c = lax.axis_index("col")
     x, core = c // 2, c % 2
@@ -131,6 +143,7 @@
     def pair(p, step):
         return left_copy(p, 2 * lax.rem(x + step, chips) + core, twin, pair_send.at[step, p])
 
+    loads[0].wait()
     for i in range(i_count):
         row_valid[pl.ds(i, 1), :] = jnp.full((1, hidden), mask_ref[z * i_count + i].astype(F32))
 
@@ -139,6 +152,8 @@
         act = sigmoid(both[:, hidden:]) * both[:, :hidden] * mask
         return act.astype(BF16).reshape(piece, i_count, hidden)
 
+    for at in (2, 3, 1, 5, 4):
+        loads[at].wait()
     gain, bias = gain_ref[...], bias_ref[...]
     for p in range(PIECES):
         values = jnp.concatenate(
@@ -168,6 +183,8 @@
         deliver(p, z)
 
     tri[...] = jnp.zeros_like(tri)
+    for at in (6, 7, 8, 9):
+        loads[at].wait()
     flat = GROUP * k_count
 
     def make_gate(g, carry):
@@ -296,9 +313,19 @@
         flat = pl.pallas_call(
             functools.partial(kernel, rows, cols),
             out_shape=jax.ShapeDtypeStruct((i_count * k_count, channels), F32),
-            in_specs=[pl.BlockSpec(memory_space=pltpu.SMEM)] + [vmem] * 9,
+            in_specs=[pl.BlockSpec(memory_space=pl.ANY)] * 10,
             out_specs=vmem,
             scratch_shapes=[
+                pltpu.SMEM(residue_mask.shape, jnp.int32),
+                pltpu.VMEM((i_count * k_count, channels), F32),
+                pltpu.VMEM((1, channels), F32),
+                pltpu.VMEM((1, channels), F32),
+                pltpu.VMEM(w_left.shape, BF16),
+                pltpu.VMEM(w_right.shape, BF16),
+                pltpu.VMEM(w_gate.shape, BF16),
+                pltpu.VMEM((1, hidden), F32),
+                pltpu.VMEM((1, hidden), F32),
+                pltpu.VMEM(w_out.shape, BF16),
                 pltpu.VMEM((rows, k_count, i_count, hidden), BF16),
                 pltpu.VMEM((cols, ratio, k_count, i_count, hidden), BF16),
                 pltpu.VMEM((cols, k_count, i_count, hidden), BF16),
@@ -315,9 +342,10 @@
                 dma((cols // 2 - 1, PIECES)),
                 dma((cols // 2, PIECES)),
                 dma((cols, PIECES)),
+                dma((10,)),
             ],
             compiler_params=pltpu.CompilerParams(
-                collective_id=0, has_side_effects=True, vmem_limit_bytes=48 * 1024 * 1024
+                collective_id=0, has_side_effects=True, vmem_limit_bytes=60 * 1024 * 1024
             ),
         )(
             residue_mask,

time: 38.6 us -> 34.9 us (0.904)
  the two profiles are of different devices: /device:TPU:24 before, /device:TPU:3 now
where the time goes in v2:
time: 34.9 us; the launch traced here: 34.2 us
  Pallas kernels  32.3 us (93%)
  local copies, waits for them, and re-layouts  1.87 us (5%)
    pallas_call x1, Pallas kernels, body(): pl.pallas_call(functools.partial(kernel, rows, cols), out_shape=jax.Shape...  32.3 us
    unnamed x1, local copies, waits for them, and re-layouts  1.87 us

profile of v2, /device:TPU:3, one launch (start us, length us, event | category | flops | bytes accessed | tf_op | source)
XLA Modules:
  0.0 34.2 jit_solution(6485264705126740272)
XLA Ops:
  0.0 32.3 %shard_map.100 = f32[1024,128]{1,0:T(8,128)} custom-call(s32[128]{0:T(128)} %refs_0_.1, f32[1024,128]{1,0:T(8,128)} %bitcast.7, f32[1,128]{1,0:T(1,128)} %bitcast.8, f32[1,128]{1,0:T(1,128)} %bitcast.9, bf16[128,256]{1,0:T(8,128)(2,1)} %refs_4_.1, bf16[128,256]{1,0:T(8,128)(2,1)} %refs_5_.1, bf16[128,128]{1,0:T(8,128)(2,1)} %refs_6_.1, f32[1,128]{1,0:T(1,128)} %bitcast.10, ...), custom_call_target="tpu_custom_call" | custom-call | tf_op jit(solution)/shard_map/pallas_call | solution.py:313
  32.4 1.9 %copy.12 = f32[32,32,128]{2,1,0:T(8,128)} copy(f32[32,32,128]{2,1,0:T(8,128)} %bitcast.6) | data formatting | bytes 1048576

commit v3 on v2

--- a/solution.py
+++ b/solution.py
@@ -29,7 +29,7 @@
     cols,
     *refs,
 ):
-    sources, out_ref, held = refs[:10], refs[10], refs[11:21]
+    sources, (out_ref, gate_ref), held = refs[:9], refs[9:11], refs[11:20]
     (
         mask_ref,
         x_ref,
@@ -40,7 +40,6 @@
         w_gate_ref,
         out_gain_ref,
         out_bias_ref,
-        w_out_ref,
     ) = held
     (
         chain,
@@ -60,12 +59,12 @@
         pair_send,
         left_recv,
         load_sem,
-    ) = refs[21:]
+    ) = refs[20:]
     loads = [
         pltpu.make_async_copy(source, target, load_sem.at[at])
         for at, (source, target) in enumerate(zip(sources, held))
     ]
-    for at in (1, 0, 5, 2, 3, 4, 6, 7, 8, 9):
+    for at in (1, 0, 5, 2, 3, 4, 6, 7, 8):
         loads[at].start()
     z = lax.axis_index("row")
     c = lax.axis_index("col")
@@ -183,7 +182,7 @@
         deliver(p, z)
 
     tri[...] = jnp.zeros_like(tri)
-    for at in (6, 7, 8, 9):
+    for at in (6, 7, 8):
         loads[at].wait()
     flat = GROUP * k_count
 
@@ -194,6 +193,8 @@
         return carry
 
     lax.fori_loop(0, i_count // GROUP, make_gate, 0)
+    gate_copy = pltpu.make_async_copy(gate, gate_ref, load_sem.at[0])
+    gate_copy.start()
 
     def relay(step, p):
         @pl.when(z - 1 - step >= 0)
@@ -218,7 +219,7 @@
 
             deliver(p, z + 1 + step)
 
-        if step == 0:
+        if step == rows - 2:
             for other in range(1, chips):
                 pair(p, other).wait_recv()
                 pair(p, other).start()
@@ -272,11 +273,11 @@
     def finish(g, carry):
         span = pl.ds(pl.multiple_of(g * flat, flat), flat)
         values = tri[pl.ds(g * GROUP, GROUP)].reshape(flat, hidden)
-        normed = layer_norm(values, out_gain_ref[...], out_bias_ref[...]).astype(BF16)
-        out_ref[span, :] = gate[span, :] * jnp.dot(normed, w_out_ref[...], preferred_element_type=F32)
+        out_ref[span, :] = layer_norm(values, out_gain_ref[...], out_bias_ref[...]).astype(BF16)
         return carry
 
     lax.fori_loop(0, i_count // GROUP, finish, 0)
+    gate_copy.wait()
 
     for p in range(PIECES):
         for step in range(rows - 1):
@@ -310,11 +311,14 @@
         piece = k_count // PIECES
         dma = pltpu.SemaphoreType.DMA
         vmem = pl.BlockSpec(memory_space=pltpu.VMEM)
-        flat = pl.pallas_call(
+        tri_norm, gate = pl.pallas_call(
             functools.partial(kernel, rows, cols),
-            out_shape=jax.ShapeDtypeStruct((i_count * k_count, channels), F32),
-            in_specs=[pl.BlockSpec(memory_space=pl.ANY)] * 10,
-            out_specs=vmem,
+            out_shape=(
+                jax.ShapeDtypeStruct((i_count * k_count, hidden), BF16),
+                jax.ShapeDtypeStruct((i_count * k_count, channels), F32),
+            ),
+            in_specs=[pl.BlockSpec(memory_space=pl.ANY)] * 9,
+            out_specs=(vmem, pl.BlockSpec(memory_space=pl.ANY)),
             scratch_shapes=[
                 pltpu.SMEM(residue_mask.shape, jnp.int32),
                 pltpu.VMEM((i_count * k_count, channels), F32),
@@ -325,7 +329,6 @@
                 pltpu.VMEM(w_gate.shape, BF16),
                 pltpu.VMEM((1, hidden), F32),
                 pltpu.VMEM((1, hidden), F32),
-                pltpu.VMEM(w_out.shape, BF16),
                 pltpu.VMEM((rows, k_count, i_count, hidden), BF16),
                 pltpu.VMEM((cols, ratio, k_count, i_count, hidden), BF16),
                 pltpu.VMEM((cols, k_count, i_count, hidden), BF16),
@@ -342,7 +345,7 @@
                 dma((cols // 2 - 1, PIECES)),
                 dma((cols // 2, PIECES)),
                 dma((cols, PIECES)),
-                dma((10,)),
+                dma((9,)),
             ],
             compiler_params=pltpu.CompilerParams(
                 collective_id=0, has_side_effects=True, vmem_limit_bytes=60 * 1024 * 1024
@@ -357,8 +360,8 @@
             w_gate,
             out_gain.reshape(1, hidden),
             out_bias.reshape(1, hidden),
-            w_out,
-        )
+        )
+        flat = gate * jnp.dot(tri_norm, w_out, preferred_element_type=F32)
         return flat.reshape(i_count, k_count, channels)
 
     placed = (P(("parts", "row"), "col", None), P("parts"), P(), P(), P(), P(), P(), P(), P(), P())

time: 34.9 us -> 31.7 us (0.908); the launches traced: 34.2 us -> 31.5 us
  Pallas kernels: 32.3 us -> 29.4 us
  matrix products: 0 us -> 2.12 us
  local copies, waits for them, and re-layouts: 1.87 us -> 0.01 us
    pallas_call x1, Pallas kernels: 32.3 us -> 29.4 us  [body(): pl.pallas_call(functools.partial(kernel, rows, cols), out_shape=(jax.Shap...]
    dot_general x0 -> x1, matrix products: none -> 2.12 us  [body(): flat = gate * jnp.dot(tri_norm, w_out, preferred_element_type=F32)]
    unnamed x1 -> x2, local copies, waits for them, and re-layouts: 1.87 us -> 0.01 us
where the time goes in v3:
time: 31.7 us; the launch traced here: 31.5 us
  Pallas kernels  29.4 us (93%)
  matrix products  2.12 us (7%)
    pallas_call x1, Pallas kernels, body(): pl.pallas_call(functools.partial(kernel, rows, cols), out_shape=(jax.Shap...  29.4 us
    dot_general x1, matrix products, body(): flat = gate * jnp.dot(tri_norm, w_out, preferred_element_type=F32)  2.12 us

profile of v3, /device:TPU:3, one launch (start us, length us, event | category | flops | bytes accessed | tf_op | source)
XLA Modules:
  0.0 31.5 jit_solution(13375137457756583444)
XLA Ops:
  0.0 0.0 copy-start
  0.0 29.4 %shard_map.100 = (bf16[1024,128]{1,0:T(8,128)(2,1)}, f32[1024,128]{1,0:T(8,128)}) custom-call(s32[128]{0:T(128)} %refs_0_.1, f32[1024,128]{1,0:T(8,128)} %bitcast.8, f32[1,128]{1,0:T(1,128)} %bitcast.9, f32[1,128]{1,0:T(1,128)} %bitcast.10, bf16[128,256]{1,0:T(8,128)(2,1)} %refs_4_.1, bf16[128,256]{1,0:T(8,128)(2,1)} %refs_5_.1, bf16[128,128]{1,0:T(8,128)(2,1)} %refs_6_.1, ...), custom_call_target="tpu_custom_call" | custom-call | tf_op jit(solution)/shard_map/pallas_call | solution.py:314
  29.4 0.0 copy-done
  29.4 2.1 %convolution_multiply_fusion = f32[1024,128]{1,0:T(8,128)} fusion(f32[1024,128]{1,0:T(8,128)} %get-tuple-element.7, bf16[1024,128]{1,0:T(8,128)(2,1)} %get-tuple-element.8, bf16[128,128]{1,0:T(8,128)(2,1)S(1)} %copy-done), kind=kOutput, calls=%fused_computation | convolution fusion | flops 33685504 | bytes 1343488 | tf_op jit(solution)/shard_map/dot_general | solution.py:364
Async XLA Ops:
  0.0 29.4 %copy-start = (bf16[128,128]{1,0:T(8,128)(2,1)S(1)}, bf16[128,128]{1,0:T(8,128)(2,1)}, u32[]{:S(2)}) copy-start(bf16[128,128]{1,0:T(8,128)(2,1)} %param.19) | copy-start | bytes 98308

commit v4 on v3

--- a/solution.py
+++ b/solution.py
@@ -9,7 +9,8 @@
 
 F32 = jnp.float32
 BF16 = jnp.bfloat16
-PIECES = 4
+SHARES = (2, 2, 2, 2)
+PIECES = len(SHARES)
 GROUP = 8
 
 
@@ -73,8 +74,8 @@
     chips = cols // 2
     ratio = rows // cols
     k_count, i_count, hidden = chain.shape[1:]
-    piece = k_count // PIECES
-    j_count = ratio * i_count
+    sizes = [share * k_count // sum(SHARES) for share in SHARES]
+    starts = [sum(sizes[:p]) for p in range(PIECES)]
 
     barrier = pltpu.get_barrier_semaphore()
 
@@ -92,7 +93,7 @@
         )
 
     def part(p):
-        return pl.ds(p * piece, piece)
+        return pl.ds(starts[p], sizes[p])
 
     def up(step, p, block):
         ref = chain.at[block, part(p)]
@@ -149,17 +150,17 @@
     def side(normed, weight, mask):
         both = jnp.dot(normed, weight, preferred_element_type=F32)
         act = sigmoid(both[:, hidden:]) * both[:, :hidden] * mask
-        return act.astype(BF16).reshape(piece, i_count, hidden)
+        return act.astype(BF16).reshape(-1, i_count, hidden)
 
     for at in (2, 3, 1, 5, 4):
         loads[at].wait()
     gain, bias = gain_ref[...], bias_ref[...]
     for p in range(PIECES):
         values = jnp.concatenate(
-            [x_ref[pl.ds(p * piece + k, i_count, stride=k_count), :] for k in range(piece)], axis=0
+            [x_ref[pl.ds(starts[p] + k, i_count, stride=k_count), :] for k in range(sizes[p])], axis=0
         )
         mask = jnp.concatenate(
-            [row_valid[...] * mask_ref[c * k_count + p * piece + k].astype(F32) for k in range(piece)], axis=0
+            [row_valid[...] * mask_ref[c * k_count + starts[p] + k].astype(F32) for k in range(sizes[p])], axis=0
         )
         normed = layer_norm(values, gain, bias).astype(BF16)
         chain[z, part(p)] = side(normed, w_right_ref[...], mask)
@@ -189,16 +190,13 @@
     def make_gate(g, carry):
         span = pl.ds(pl.multiple_of(g * flat, flat), flat)
         normed = layer_norm(x_ref[span, :], gain, bias).astype(BF16)
-        gate[span, :] = sigmoid(jnp.dot(normed, w_gate_ref[...], preferred_element_type=F32))
+        gate_ref[span, :] = sigmoid(jnp.dot(normed, w_gate_ref[...], preferred_element_type=F32))
         return carry
 
     lax.fori_loop(0, i_count // GROUP, make_gate, 0)
-    gate_copy = pltpu.make_async_copy(gate, gate_ref, load_sem.at[0])
-    gate_copy.start()
 
     def relay(step, p):
-        @pl.when(z - 1 - step >= 0)
-        def _():
+        def upward():
             up(step, p, z - 1 - step).wait_recv()
             if step < rows - 2:
 
@@ -208,6 +206,8 @@
 
             deliver(p, z - 1 - step)
 
+        pl.when((z - 1 - step >= 0) & (2 * z >= rows))(upward)
+
         @pl.when(z + 1 + step < rows)
         def _():
             down(step, p, z + 1 + step).wait_recv()
@@ -218,6 +218,8 @@
                     down(step + 1, p, z + 1 + step).start()
 
             deliver(p, z + 1 + step)
+
+        pl.when((z - 1 - step >= 0) & (2 * z < rows))(upward)
 
         if step == rows - 2:
             for other in range(1, chips):
@@ -233,6 +235,8 @@
             owner = 2 * lax.rem(x + other, chips) + 1 - core
             left_copy(p, owner, twin, pair_send.at[other, p]).wait_recv()
 
+        piece = sizes[p]
+
         def widen(owner, carry):
             left32[pl.ds(owner * piece, piece)] = left[owner, part(p)].astype(F32)
             return carry
@@ -246,7 +250,7 @@
 
             def add(owner, sums):
                 for k in range(piece):
-                    other = right[owner, offset, p * piece + k].astype(F32)
+                    other = right[owner, offset, starts[p] + k].astype(F32)
                     sums = tuple(
                         total + left32[owner * piece + k, pl.ds(first + g, 1), :] * other
                         for g, total in enumerate(sums)
@@ -277,7 +281,6 @@
         return carry
 
     lax.fori_loop(0, i_count // GROUP, finish, 0)
-    gate_copy.wait()
 
     for p in range(PIECES):
         for step in range(rows - 1):
@@ -308,17 +311,17 @@
         i_count, k_count, channels = pair_acts.shape
         hidden = w_out.shape[0]
         ratio = rows // cols
-        piece = k_count // PIECES
+        piece = max(SHARES) * k_count // sum(SHARES)
         dma = pltpu.SemaphoreType.DMA
         vmem = pl.BlockSpec(memory_space=pltpu.VMEM)
         tri_norm, gate = pl.pallas_call(
             functools.partial(kernel, rows, cols),
             out_shape=(
-                jax.ShapeDtypeStruct((i_count * k_count, hidden), BF16),
-                jax.ShapeDtypeStruct((i_count * k_count, channels), F32),
+                pltpu.VMEM((i_count * k_count, hidden), BF16),
+                pltpu.VMEM((i_count * k_count, channels), F32),
             ),
             in_specs=[pl.BlockSpec(memory_space=pl.ANY)] * 9,
-            out_specs=(vmem, pl.BlockSpec(memory_space=pl.ANY)),
+            out_specs=(vmem, vmem),
             scratch_shapes=[
                 pltpu.SMEM(residue_mask.shape, jnp.int32),
                 pltpu.VMEM((i_count * k_count, channels), F32),

time: 31.7 us -> 29.9 us (0.943)
  matrix products: 2.12 us -> 1.01 us
  Pallas kernels: 29.4 us -> 28.7 us
    dot_general x1, matrix products: 2.12 us -> 1.01 us  [body(): flat = gate * jnp.dot(tri_norm, w_out, preferred_element_type=F32)]
    pallas_call x1, Pallas kernels: 29.4 us -> 28.7 us  [body(): pl.pallas_call(functools.partial(kernel, rows, cols), out_shape=(pltpu.VM...]
where the time goes in v4:
time: 29.9 us; the launch traced here: 29.7 us
  Pallas kernels  28.7 us (96%)
  matrix products  1.01 us (3%)
    pallas_call x1, Pallas kernels, body(): pl.pallas_call(functools.partial(kernel, rows, cols), out_shape=(pltpu.VM...  28.7 us
    dot_general x1, matrix products, body(): flat = gate * jnp.dot(tri_norm, w_out, preferred_element_type=F32)  1.01 us

profile of v4, /device:TPU:3, one launch (start us, length us, event | category | flops | bytes accessed | tf_op | source)
XLA Modules:
  0.0 29.7 jit_solution(1118843023868690610)
XLA Ops:
  0.0 0.0 copy-start
  0.0 28.7 %shard_map.100 = (bf16[1024,128]{1,0:T(8,128)(2,1)S(1)}, f32[1024,128]{1,0:T(8,128)S(1)}) custom-call(s32[128]{0:T(128)} %refs_0_.1, f32[1024,128]{1,0:T(8,128)} %bitcast.8, f32[1,128]{1,0:T(1,128)} %bitcast.9, f32[1,128]{1,0:T(1,128)} %bitcast.10, bf16[128,256]{1,0:T(8,128)(2,1)} %refs_4_.1, bf16[128,256]{1,0:T(8,128)(2,1)} %refs_5_.1, ...), custom_call_target="tpu_custom_call" | custom-call | tf_op jit(solution)/shard_map/pallas_call | solution.py:317
  28.7 0.0 copy-done
  28.7 1.0 %convolution_multiply_fusion = f32[1024,128]{1,0:T(8,128)} fusion(f32[1024,128]{1,0:T(8,128)S(1)} %get-tuple-element.7, bf16[1024,128]{1,0:T(8,128)(2,1)S(1)} %get-tuple-element.8, bf16[128,128]{1,0:T(8,128)(2,1)S(1)} %copy-done), kind=kOutput, calls=%fused_computation | convolution fusion | flops 33685504 | bytes 1343488 | tf_op jit(solution)/shard_map/dot_general | solution.py:367
Async XLA Ops:
  0.0 28.7 %copy-start = (bf16[128,128]{1,0:T(8,128)(2,1)S(1)}, bf16[128,128]{1,0:T(8,128)(2,1)}, u32[]{:S(2)}) copy-start(bf16[128,128]{1,0:T(8,128)(2,1)} %param.19) | copy-start | bytes 98308

commit v5 on v4

--- a/solution.py
+++ b/solution.py
@@ -226,29 +226,35 @@
                 pair(p, other).wait_recv()
                 pair(p, other).start()
 
-    def multiply(p):
-        for owner in range(cols):
+    def multiply(p, others):
+        owners = [2 * lax.rem(x + other, chips) + side_core for other in others for side_core in range(2)]
+        for owner in owners:
             for offset in range(ratio):
                 ref = right.at[owner, offset, part(p)]
                 pltpu.make_async_copy(ref, ref, swap_recv.at[owner, offset, p]).wait()
-        for other in range(chips):
+        for other in others:
             owner = 2 * lax.rem(x + other, chips) + 1 - core
             left_copy(p, owner, twin, pair_send.at[other, p]).wait_recv()
 
         piece = sizes[p]
 
-        def widen(owner, carry):
+        def owner_at(at):
+            return lax.rem(2 * (x + others[0]) + at, cols)
+
+        def widen(at, carry):
+            owner = owner_at(at)
             left32[pl.ds(owner * piece, piece)] = left[owner, part(p)].astype(F32)
             return carry
 
-        lax.fori_loop(0, cols, widen, 0)
+        lax.fori_loop(0, len(owners), widen, 0)
         groups = i_count // GROUP
 
         def block(at, carry):
             offset, first = at // groups, pl.multiple_of((at % groups) * GROUP, GROUP)
             js = pl.ds(pl.multiple_of(offset * i_count, i_count), i_count)
 
-            def add(owner, sums):
+            def add(at, sums):
+                owner = owner_at(at)
                 for k in range(piece):
                     other = right[owner, offset, starts[p] + k].astype(F32)
                     sums = tuple(
@@ -258,7 +264,7 @@
                 return sums
 
             sums = tuple(tri[first + g, js, :] for g in range(GROUP))
-            sums = lax.fori_loop(0, cols, add, sums)
+            sums = lax.fori_loop(0, len(owners), add, sums)
             for g in range(GROUP):
                 tri[first + g, js, :] = sums[g]
             return carry
@@ -271,8 +277,9 @@
     for p in range(PIECES):
         relay(rows - 2, p)
         if p > 0:
-            multiply(p - 1)
-    multiply(PIECES - 1)
+            multiply(p - 1, range(chips))
+    multiply(PIECES - 1, range(1))
+    multiply(PIECES - 1, range(1, chips))
 
     def finish(g, carry):
         span = pl.ds(pl.multiple_of(g * flat, flat), flat)

time: 29.9 us -> 30.4 us (1.017)
  Pallas kernels: 28.7 us -> 29.2 us
    pallas_call x1, Pallas kernels: 28.7 us -> 29.2 us  [body(): pl.pallas_call(functools.partial(kernel, rows, cols), out_shape=(pltpu.VM...]
where the time goes in v5:
time: 30.4 us; the launch traced here: 30.3 us
  Pallas kernels  29.2 us (96%)
  matrix products  1.01 us (3%)
    pallas_call x1, Pallas kernels, body(): pl.pallas_call(functools.partial(kernel, rows, cols), out_shape=(pltpu.VM...  29.2 us
    dot_general x1, matrix products, body(): flat = gate * jnp.dot(tri_norm, w_out, preferred_element_type=F32)  1.01 us

profile of v5, /device:TPU:3, one launch (start us, length us, event | category | flops | bytes accessed | tf_op | source)
XLA Modules:
  0.0 30.3 jit_solution(3405715596480773593)
XLA Ops:
  0.0 0.0 copy-start
  0.0 29.2 %shard_map.100 = (bf16[1024,128]{1,0:T(8,128)(2,1)S(1)}, f32[1024,128]{1,0:T(8,128)S(1)}) custom-call(s32[128]{0:T(128)} %refs_0_.1, f32[1024,128]{1,0:T(8,128)} %bitcast.8, f32[1,128]{1,0:T(1,128)} %bitcast.9, f32[1,128]{1,0:T(1,128)} %bitcast.10, bf16[128,256]{1,0:T(8,128)(2,1)} %refs_4_.1, bf16[128,256]{1,0:T(8,128)(2,1)} %refs_5_.1, ...), custom_call_target="tpu_custom_call" | custom-call | tf_op jit(solution)/shard_map/pallas_call | solution.py:324
  29.2 0.0 copy-done
  29.2 1.0 %convolution_multiply_fusion = f32[1024,128]{1,0:T(8,128)} fusion(f32[1024,128]{1,0:T(8,128)S(1)} %get-tuple-element.7, bf16[1024,128]{1,0:T(8,128)(2,1)S(1)} %get-tuple-element.8, bf16[128,128]{1,0:T(8,128)(2,1)S(1)} %copy-done), kind=kOutput, calls=%fused_computation | convolution fusion | flops 33685504 | bytes 1343488 | tf_op jit(solution)/shard_map/dot_general | solution.py:374
Async XLA Ops:
  0.0 29.2 %copy-start = (bf16[128,128]{1,0:T(8,128)(2,1)S(1)}, bf16[128,128]{1,0:T(8,128)(2,1)}, u32[]{:S(2)}) copy-start(bf16[128,128]{1,0:T(8,128)(2,1)} %param.19) | copy-start | bytes 98308
